TPU v7x, 512 devices: a whole 4x8x8 slice. The times are simulated.
512 devices in a mesh: ens: 4 (over y_hi), lat: 8 (over y_lo, x), lon: 16 (over z, core).
Axes of the slice: x: 4, y: 8 (y_hi: 4, y_lo: 2; y = y_hi * 2 + y_lo), z: 8, core: 2. Of those that a mesh axis runs over, the one named last changes fastest.
Arguments:
- initial_state: float32 [24, 128, 2048], P('ens', 'lat', 'lon'), parts along dimension 0, may hold values from -6 to 6
- diffusion: float32 [128, 2048], P('lat', 'lon'), may hold values from 0.05 to 0.2
- mixing: float32 [6, 6], replicated, may hold values from -0.3 to 0.3
- land_mask: int32 [128, 2048], P('lat', 'lon'), may hold values 0 or 1
- first_layer: bfloat16 [128, 54], replicated, may hold values from -0.875 to 0.875
- second_layer: bfloat16 [128, 128], replicated, may hold values from -0.5 to 0.5
- output_layer: bfloat16 [6, 128], replicated, may hold values from -0.5 to 0.5
- cotangent: float32 [24, 128, 2048], P('ens', 'lat', 'lon'), parts along dimension 0, may hold values from -20 to 20
- update_noise: float32 [96256], P('ens'), parts along dimension 0, may hold values from -0.15 to 0.15
Outputs:
- final_state: float32 [24, 128, 2048], P('ens', 'lat', 'lon'), parts along dimension 0
- initial_adjoint: float32 [24, 128, 2048], P('ens', 'lat', 'lon'), parts along dimension 0
- new_params: float32 [96256], P('ens'), parts along dimension 0
- noise_ratio: float32 [4], P('ens'), parts along dimension 0
There are 4 independent parts, one for each index of `ens`. A program takes and returns all parts, laid end to end along the dimension named above; an argument that names none is the same for every part. Nothing has to cross between parts.
All inputs are finite; a program needn't handle non-finite values. No bound on the sum of `land_mask` on one device may be relied on, other than what follows from the above.
Results may differ from a plain program's by a relative error of at most 0.0033.
Values sent between devices are 32-bit elements; how exact they have to be, the bound alone decides.
A program may use at most 64 MiB of HBM per device.

v0:
```python
import jax
import jax.numpy as jnp
from jax import lax
from jax.sharding import PartitionSpec as P

STEPS = 2
closure_dt = 0.1
learn_rate = 0.1
epsilon = 1e-06
offsets = [(row_shift, col_shift) for row_shift in (-1, 0, 1) for col_shift in (-1, 0, 1)]


def with_halo(value, sides, width, wrap):
    for axis, dim in sides:
        devices, length = (lax.axis_size(axis), value.shape[dim])
        up = [(i, (i + 1) % devices) for i in range(devices if wrap else devices - 1)]
        down = [(j, i) for i, j in up]
        last = lax.slice_in_dim(value, length - width, length, axis=dim)
        first = lax.slice_in_dim(value, 0, width, axis=dim)
        before = lax.ppermute(last, axis, up)
        after = lax.ppermute(first, axis, down)
        value = jnp.concatenate([before, value, after], axis=dim)
    return value


def contract_last(left, right):
    return lax.dot_general(
        left, right, (((1,), (1,)), ((), ())), preferred_element_type=jnp.float32
    )


def contract_first(left, right):
    return lax.dot_general(
        left, right, (((0,), (0,)), ((), ())), preferred_element_type=jnp.float32
    )


def build_patch(slab, rows, cols):
    return jnp.concatenate(
        [
            slab[:, 1 + row_shift : 1 + row_shift + rows, 1 + col_shift : 1 + col_shift + cols]
            for row_shift, col_shift in offsets
        ],
        axis=0,
    )


def hidden_layers(flat, first_layer, second_layer):
    hidden_one = jnp.tanh(jnp.dot(first_layer, flat, preferred_element_type=jnp.float32)).astype(
        jnp.bfloat16
    )
    hidden_two = jnp.tanh(
        jnp.dot(second_layer, hidden_one, preferred_element_type=jnp.float32)
    ).astype(jnp.bfloat16)
    return (hidden_one, hidden_two)


def forward_block(slab, mask_rows, diff_rows, mixing, first_layer, second_layer, output_layer):
    fields = slab.shape[0]
    rows = slab.shape[1] - 2
    cols = slab.shape[2] - 2
    count = rows * cols
    patch = build_patch(slab, rows, cols)
    centre = patch[4 * fields : 5 * fields]
    laplace = (
        patch[fields : 2 * fields]
        + patch[3 * fields : 4 * fields]
        + patch[5 * fields : 6 * fields]
        + patch[7 * fields : 8 * fields]
        - 4.0 * centre
    )
    flat = patch.reshape(9 * fields, count).astype(jnp.bfloat16)
    hidden_one, hidden_two = hidden_layers(flat, first_layer, second_layer)
    tendency = jnp.dot(output_layer, hidden_two, preferred_element_type=jnp.float32)
    mixed = jnp.dot(mixing, centre.reshape(fields, count), precision=lax.Precision.HIGHEST)
    update = (
        centre
        + diff_rows[None] * laplace
        + (mixed + closure_dt * tendency).reshape(fields, rows, cols)
    )
    return mask_rows[None] * update


def backward_block(
    slab, adjoint_rows, mask_rows, diff_rows, mixing, first_layer, second_layer, output_layer
):
    fields = slab.shape[0]
    rows = slab.shape[1] - 2
    cols = slab.shape[2] - 2
    count = rows * cols
    patch = build_patch(slab, rows, cols)
    flat = patch.reshape(9 * fields, count).astype(jnp.bfloat16)
    hidden_one, hidden_two = hidden_layers(flat, first_layer, second_layer)
    masked = (mask_rows[None] * adjoint_rows).reshape(fields, count)
    out_grad = (closure_dt * masked).astype(jnp.bfloat16)
    back_two = (
        contract_first(output_layer, out_grad) * (1.0 - jnp.square(hidden_two.astype(jnp.float32)))
    ).astype(jnp.bfloat16)
    back_one = (
        contract_first(second_layer, back_two) * (1.0 - jnp.square(hidden_one.astype(jnp.float32)))
    ).astype(jnp.bfloat16)
    patch_grad = contract_first(first_layer, back_one)
    direct = masked + lax.dot_general(
        mixing,
        masked,
        (((0,), (0,)), ((), ())),
        precision=lax.Precision.HIGHEST,
        preferred_element_type=jnp.float32,
    )
    spread = diff_rows.reshape(1, count) * masked
    blank = jnp.zeros_like(masked)
    extra = jnp.concatenate(
        [blank, spread, blank, spread, direct - 4.0 * spread, spread, blank, spread, blank], axis=0
    )
    patch_grad = (patch_grad + extra).reshape(9 * fields, rows, cols)
    grads = jnp.concatenate(
        [
            contract_last(back_one, flat).ravel(),
            contract_last(back_two, hidden_one).ravel(),
            contract_last(out_grad, hidden_two).ravel(),
        ]
    )
    return (patch_grad, grads)


def on_device(
    initial_state,
    diffusion,
    mixing,
    land_mask,
    first_layer,
    second_layer,
    output_layer,
    cotangent,
    update_noise,
):
    fields, rows, cols = initial_state.shape
    mask = land_mask.astype(jnp.float32)
    state = initial_state
    saved = []
    for step in range(STEPS):
        wide = with_halo(state, (("lon", 2),), 1, True)
        padded = with_halo(wide, (("lat", 1),), 1, False)
        saved.append(padded)
        state = forward_block(
            padded, mask, diffusion, mixing, first_layer, second_layer, output_layer
        )
    adjoint = cotangent
    local_grad = jnp.zeros((first_layer.size + second_layer.size + output_layer.size,), jnp.float32)
    for step in reversed(range(STEPS)):
        patch_grad, grads = backward_block(
            saved[step], adjoint, mask, diffusion, mixing, first_layer, second_layer, output_layer
        )
        local_grad = local_grad + grads
        wide_grad = with_halo(patch_grad, (("lon", 2),), 1, True)
        grad_pad = with_halo(wide_grad, (("lat", 1),), 1, False)
        total = jnp.zeros((fields, rows, cols), jnp.float32)
        for number, (row_shift, col_shift) in enumerate(offsets):
            total = (
                total
                + grad_pad[
                    number * fields : (number + 1) * fields,
                    1 - row_shift : 1 - row_shift + rows,
                    1 - col_shift : 1 - col_shift + cols,
                ]
            )
        adjoint = total
    params_count = local_grad.shape[0]
    band = lax.psum(local_grad, "lon")
    total_grad, band_square = lax.psum((band, jnp.sum(band * band)), "lat")
    grad_square = jnp.sum(total_grad * total_grad)
    noise_ratio = (band_square / (grad_square + epsilon)).reshape(1)
    params = jnp.concatenate(
        [
            first_layer.astype(jnp.float32).ravel(),
            second_layer.astype(jnp.float32).ravel(),
            output_layer.astype(jnp.float32).ravel(),
        ]
    )
    new_params = (
        params
        - learn_rate * total_grad / jnp.sqrt(grad_square / params_count + epsilon)
        + update_noise
    )
    return (state, adjoint, new_params, noise_ratio)


def solution(mesh):
    placed = (
        P("ens", "lat", "lon"),
        P("lat", "lon"),
        P(),
        P("lat", "lon"),
        P(),
        P(),
        P(),
        P("ens", "lat", "lon"),
        P("ens"),
    )
    return jax.shard_map(
        on_device,
        mesh=mesh,
        in_specs=placed,
        out_specs=(P("ens", "lat", "lon"), P("ens", "lat", "lon"), P("ens"), P("ens")),
        check_vma=False,
    )
```

profile of v0, /device:TPU:40, one launch (start us, length us, event | category | flops | bytes accessed | tf_op | source)
XLA Modules:
  0.0 304.6 jit_solution(4147958158141349705)
XLA Ops:
  8.2 8.5 %collective-permute-start.1 = (f32[6,16,1]{2,1,0:T(8,128)S(1)}, f32[6,16,1]{2,1,0:T(8,128)S(1)}, u32[]{:S(2)}, u32[]{:S(2)}) collective-permute-start(f32[6,16,1]{2,1,0:T(8,128)S(1)} %get-tuple-element.31), channel_id=1, source_target_pairs={{1,0},{2,1},{3,2},{4,3},{5,4},{6,5},{7,6},{8,7},{9,8},{10,9},{11,1... | collective-permute-start | bytes 1160 | tf_op jit(solution)/shard_map/ppermute | solution.py:21
  16.7 1.8 collective-permute-done
  18.6 5.5 %collective-permute-start.3 = (f32[6,1,130]{2,1,0:T(1,128)S(1)}, f32[6,1,130]{2,1,0:T(1,128)S(1)}, u32[]{:S(2)}, u32[]{:S(2)}) collective-permute-start(f32[6,1,130]{2,1,0:T(1,128)S(1)} %get-tuple-element.26), channel_id=1, source_target_pairs={{16,0},{32,16},{48,32},{64,48},{80,64},{96,80},{112,96},{17,1},{33... | collective-permute-start | bytes 9368 | tf_op jit(solution)/shard_map/ppermute | solution.py:21
  24.0 1.9 collective-permute-start.2
  26.7 5.0 %collective-permute-done.2 = f32[6,1,130]{2,1,0:T(1,128)S(1)} collective-permute-done((f32[6,1,130]{2,1,0:T(1,128)S(1)}, f32[6,1,130]{2,1,0:T(1,128)S(1)}, u32[]{:S(2)}, u32[]{:S(2)}) %collective-permute-start.2) | collective-permute-done | bytes 3152 | tf_op jit(solution)/shard_map/ppermute | solution.py:20
  35.5 3.0 collective-permute-start.5
  40.4 1.9 collective-permute-start.7
  42.3 3.9 %collective-permute-start.6 = (f32[6,1,130]{2,1,0:T(1,128)S(1)}, f32[6,1,130]{2,1,0:T(1,128)S(1)}, u32[]{:S(2)}, u32[]{:S(2)}) collective-permute-start(f32[6,1,130]{2,1,0:T(1,128)S(1)} %get-tuple-element.23), channel_id=1, source_target_pairs={{0,16},{16,32},{32,48},{48,64},{64,80},{80,96},{96,112},{1,17},{17... | collective-permute-start | bytes 9368 | tf_op jit(solution)/shard_map/ppermute | solution.py:20
  46.5 3.5 %collective-permute-done.6 = f32[6,1,130]{2,1,0:T(1,128)S(1)} collective-permute-done((f32[6,1,130]{2,1,0:T(1,128)S(1)}, f32[6,1,130]{2,1,0:T(1,128)S(1)}, u32[]{:S(2)}, u32[]{:S(2)}) %collective-permute-start.6) | collective-permute-done | bytes 3152 | tf_op jit(solution)/shard_map/ppermute | solution.py:20
  56.4 11.9 %concatenate.120 = f32[54,2048]{1,0:T(8,128)} concatenate(f32[6,2048]{1,0:T(8,128)S(1)} %broadcast.26, f32[6,2048]{1,0:T(8,128)S(1)} %bitcast_multiply_fusion.2, f32[6,2048]{1,0:T(8,128)S(1)} %broadcast.26, f32[6,2048]{1,0:T(8,128)S(1)} %bitcast_multiply_fusion.2, f32[6,2048]{1,0:T(8,128)} %fusion.13, f32[6,2048]{1,0:T(8,128)S(1)} %bitcast_multiply_fusion.2, ...), dimensions={0} | concatenate | bytes 884736 | tf_op jit(solution)/shard_map/concatenate | solution.py:112
  70.0 2.9 collective-permute-start.9
  74.0 5.0 %collective-permute-done.8 = f32[54,16,1]{2,1,0:T(8,128)S(1)} collective-permute-done((f32[54,16,1]{2,1,0:T(8,128)S(1)}, f32[54,16,1]{2,1,0:T(8,128)S(1)}, u32[]{:S(2)}, u32[]{:S(2)}) %collective-permute-start.8) | collective-permute-done | bytes 3488 | tf_op jit(solution)/shard_map/ppermute | solution.py:20
  80.0 2.0 collective-permute-start.10
  82.1 4.1 %collective-permute-start.11 = (f32[54,1,130]{2,1,0:T(1,128)}, f32[54,1,130]{2,1,0:T(1,128)}, u32[]{:S(2)}, u32[]{:S(2)}) collective-permute-start(f32[54,1,130]{2,1,0:T(1,128)} %get-tuple-element.15), channel_id=1, source_target_pairs={{0,16},{16,32},{32,48},{48,64},{64,80},{80,96},{96,112},{1,17},{17... | collective-permute-start | bytes 84248 | tf_op jit(solution)/shard_map/ppermute | solution.py:20
  86.5 4.2 %collective-permute-done.11 = f32[54,1,130]{2,1,0:T(1,128)} collective-permute-done((f32[54,1,130]{2,1,0:T(1,128)}, f32[54,1,130]{2,1,0:T(1,128)}, u32[]{:S(2)}, u32[]{:S(2)}) %collective-permute-start.11) | collective-permute-done | bytes 28112 | tf_op jit(solution)/shard_map/ppermute | solution.py:20
  95.1 2.9 collective-permute-start.13
  98.8 5.3 %collective-permute-done.12 = f32[54,16,1]{2,1,0:T(8,128)S(1)} collective-permute-done((f32[54,16,1]{2,1,0:T(8,128)S(1)}, f32[54,16,1]{2,1,0:T(8,128)S(1)}, u32[]{:S(2)}, u32[]{:S(2)}) %collective-permute-start.12) | collective-permute-done | bytes 3488 | tf_op jit(solution)/shard_map/ppermute | solution.py:20
  104.5 1.9 collective-permute-start.14
  106.4 3.9 %collective-permute-start.15 = (f32[54,1,130]{2,1,0:T(1,128)S(1)}, f32[54,1,130]{2,1,0:T(1,128)S(1)}, u32[]{:S(2)}, u32[]{:S(2)}) collective-permute-start(f32[54,1,130]{2,1,0:T(1,128)S(1)} %get-tuple-element.13), channel_id=1, source_target_pairs={{0,16},{16,32},{32,48},{48,64},{64,80},{80,96},{96,112},{1,17},{17... | collective-permute-start | bytes 84248 | tf_op jit(solution)/shard_map/ppermute | solution.py:20
  110.3 93.3 %all-reduce.3.cloned.1.call-done = f32[24064]{0:T(1024)} async-done(((f32[24064]{0:T(1024)}), f32[24064]{0:T(1024)}) %all-reduce.3.cloned.1.call-update) | async-done | bytes 96272 | tf_op jit(solution)/shard_map/psum | solution.py:169
  206.8 20.1 %psum.23 = f32[]{:T(128)} all-reduce(f32[]{:T(128)} %multiply_reduce_fusion), channel_id=1, replica_groups=mesh['ens'=4,'lat'=8,'lon'=16] {'lat'}, use_global_device_ids=true, to_apply=%region_4.0 | all-reduce | flops 1 | bytes 8 | tf_op jit(solution)/shard_map/psum | solution.py:170
  226.9 64.6 %all-reduce.5.cloned.1.call-done = f32[24064]{0:T(1024)} async-done(((f32[24064]{0:T(1024)}), f32[24064]{0:T(1024)}) %all-reduce.5.cloned.1.call-update) | async-done | bytes 96272 | tf_op jit(solution)/shard_map/psum | solution.py:170
  291.5 1.5 multiply_reduce_fusion.1
  295.1 1.6 subtract_add_fusion
  (135 shorter events, 26.8 us)
Async XLA Ops:
  7.2 18.8 %copy-start = (f32[6,6]{1,0:T(8,128)S(1)}, f32[6,6]{1,0:T(8,128)}, u32[]{:S(2)}) copy-start(f32[6,6]{1,0:T(8,128)} %param.11) | copy-start | bytes 436
  7.2 11.3 %copy-start.1 = (f32[6,16,128]{2,1,0:T(8,128)S(1)}, f32[6,16,128]{2,1,0:T(8,128)}, u32[]{:S(2)}) copy-start(f32[6,16,128]{2,1,0:T(8,128)} %param.9) | copy-start | bytes 147460
  7.2 196.4 %all-reduce.3.cloned.1.call-start = ((), (), s32[]{:S(2)}) async-start(), calls=%async_computation | async-start | bytes 196608 | tf_op jit(solution)/shard_map/psum | solution.py:169
  8.2 10.3 %collective-permute-start = (f32[6,16,1]{2,1,0:T(8,128)S(1)}, f32[6,16,1]{2,1,0:T(8,128)S(1)}, u32[]{:S(2)}, u32[]{:S(2)}) collective-permute-start(f32[6,16,1]{2,1,0:T(8,128)S(1)} %get-tuple-element.30), channel_id=1, source_target_pairs={{0,1},{1,2},{2,3},{3,4},{4,5},{5,6},{6,7},{7,8},{8,9},{9,10},{10,1... | collective-permute-start | bytes 1160 | tf_op jit(solution)/shard_map/ppermute | solution.py:20
  8.2 10.2 %collective-permute-start.1 = (f32[6,16,1]{2,1,0:T(8,128)S(1)}, f32[6,16,1]{2,1,0:T(8,128)S(1)}, u32[]{:S(2)}, u32[]{:S(2)}) collective-permute-start(f32[6,16,1]{2,1,0:T(8,128)S(1)} %get-tuple-element.31), channel_id=1, source_target_pairs={{1,0},{2,1},{3,2},{4,3},{5,4},{6,5},{7,6},{8,7},{9,8},{10,9},{11,1... | collective-permute-start | bytes 1160 | tf_op jit(solution)/shard_map/ppermute | solution.py:21
  18.6 8.1 %collective-permute-start.3 = (f32[6,1,130]{2,1,0:T(1,128)S(1)}, f32[6,1,130]{2,1,0:T(1,128)S(1)}, u32[]{:S(2)}, u32[]{:S(2)}) collective-permute-start(f32[6,1,130]{2,1,0:T(1,128)S(1)} %get-tuple-element.26), channel_id=1, source_target_pairs={{16,0},{32,16},{48,32},{64,48},{80,64},{96,80},{112,96},{17,1},{33... | collective-permute-start | bytes 9368 | tf_op jit(solution)/shard_map/ppermute | solution.py:21
  24.0 7.6 %collective-permute-start.2 = (f32[6,1,130]{2,1,0:T(1,128)S(1)}, f32[6,1,130]{2,1,0:T(1,128)S(1)}, u32[]{:S(2)}, u32[]{:S(2)}) collective-permute-start(f32[6,1,130]{2,1,0:T(1,128)S(1)} %get-tuple-element.27), channel_id=1, source_target_pairs={{0,16},{16,32},{32,48},{48,64},{64,80},{80,96},{96,112},{1,17},{17... | collective-permute-start | bytes 9368 | tf_op jit(solution)/shard_map/ppermute | solution.py:20
  26.7 25.1 %copy-start.14 = (f32[16,128]{1,0:T(8,128)}, f32[16,128]{1,0:T(8,128)S(1)}, u32[]{:S(2)}) copy-start(f32[16,128]{1,0:T(8,128)S(1)} %convert_element_type.70) | copy-start | bytes 24580
  35.5 4.7 %collective-permute-start.4 = (f32[6,16,1]{2,1,0:T(8,128)S(1)}, f32[6,16,1]{2,1,0:T(8,128)S(1)}, u32[]{:S(2)}, u32[]{:S(2)}) collective-permute-start(f32[6,16,1]{2,1,0:T(8,128)S(1)} %get-tuple-element.28), channel_id=1, source_target_pairs={{0,1},{1,2},{2,3},{3,4},{4,5},{5,6},{6,7},{7,8},{8,9},{9,10},{10,1... | collective-permute-start | bytes 1160 | tf_op jit(solution)/shard_map/ppermute | solution.py:20
  35.5 4.7 %collective-permute-start.5 = (f32[6,16,1]{2,1,0:T(8,128)S(1)}, f32[6,16,1]{2,1,0:T(8,128)S(1)}, u32[]{:S(2)}, u32[]{:S(2)}) collective-permute-start(f32[6,16,1]{2,1,0:T(8,128)S(1)} %get-tuple-element.29), channel_id=1, source_target_pairs={{1,0},{2,1},{3,2},{4,3},{5,4},{6,5},{7,6},{8,7},{9,8},{10,9},{11,1... | collective-permute-start | bytes 1160 | tf_op jit(solution)/shard_map/ppermute | solution.py:21
  40.4 6.1 %collective-permute-start.7 = (f32[6,1,130]{2,1,0:T(1,128)S(1)}, f32[6,1,130]{2,1,0:T(1,128)S(1)}, u32[]{:S(2)}, u32[]{:S(2)}) collective-permute-start(f32[6,1,130]{2,1,0:T(1,128)S(1)} %get-tuple-element.22), channel_id=1, source_target_pairs={{16,0},{32,16},{48,32},{64,48},{80,64},{96,80},{112,96},{17,1},{33... | collective-permute-start | bytes 9368 | tf_op jit(solution)/shard_map/ppermute | solution.py:21
  42.3 7.6 %collective-permute-start.6 = (f32[6,1,130]{2,1,0:T(1,128)S(1)}, f32[6,1,130]{2,1,0:T(1,128)S(1)}, u32[]{:S(2)}, u32[]{:S(2)}) collective-permute-start(f32[6,1,130]{2,1,0:T(1,128)S(1)} %get-tuple-element.23), channel_id=1, source_target_pairs={{0,16},{16,32},{32,48},{48,64},{64,80},{80,96},{96,112},{1,17},{17... | collective-permute-start | bytes 9368 | tf_op jit(solution)/shard_map/ppermute | solution.py:20
  70.0 8.9 %collective-permute-start.8 = (f32[54,16,1]{2,1,0:T(8,128)S(1)}, f32[54,16,1]{2,1,0:T(8,128)S(1)}, u32[]{:S(2)}, u32[]{:S(2)}) collective-permute-start(f32[54,16,1]{2,1,0:T(8,128)S(1)} %get-tuple-element.18), channel_id=1, source_target_pairs={{0,1},{1,2},{2,3},{3,4},{4,5},{5,6},{6,7},{7,8},{8,9},{9,10},{10,1... | collective-permute-start | bytes 10376 | tf_op jit(solution)/shard_map/ppermute | solution.py:20
  70.0 8.9 %collective-permute-start.9 = (f32[54,16,1]{2,1,0:T(8,128)S(1)}, f32[54,16,1]{2,1,0:T(8,128)S(1)}, u32[]{:S(2)}, u32[]{:S(2)}) collective-permute-start(f32[54,16,1]{2,1,0:T(8,128)S(1)} %get-tuple-element.19), channel_id=1, source_target_pairs={{1,0},{2,1},{3,2},{4,3},{5,4},{6,5},{7,6},{8,7},{9,8},{10,9},{11,1... | collective-permute-start | bytes 10376 | tf_op jit(solution)/shard_map/ppermute | solution.py:21
  74.0 12.2 %copy-start.5 = (f32[1,6,16,128]{3,2,1,0:T(8,128)S(1)}, f32[1,6,16,128]{3,2,1,0:T(8,128)}, u32[]{:S(2)}) copy-start(f32[1,6,16,128]{3,2,1,0:T(8,128)} %copy-done.4) | copy-start | bytes 147460
  80.0 6.5 %collective-permute-start.10 = (f32[54,1,130]{2,1,0:T(1,128)}, f32[54,1,130]{2,1,0:T(1,128)S(1)}, u32[]{:S(2)}, u32[]{:S(2)}) collective-permute-start(f32[54,1,130]{2,1,0:T(1,128)} %get-tuple-element.14), channel_id=1, source_target_pairs={{16,0},{32,16},{48,32},{64,48},{80,64},{96,80},{112,96},{17,1},{33... | collective-permute-start | bytes 84248 | tf_op jit(solution)/shard_map/ppermute | solution.py:21
  82.1 8.6 %collective-permute-start.11 = (f32[54,1,130]{2,1,0:T(1,128)}, f32[54,1,130]{2,1,0:T(1,128)}, u32[]{:S(2)}, u32[]{:S(2)}) collective-permute-start(f32[54,1,130]{2,1,0:T(1,128)} %get-tuple-element.15), channel_id=1, source_target_pairs={{0,16},{16,32},{32,48},{48,64},{64,80},{80,96},{96,112},{1,17},{17... | collective-permute-start | bytes 84248 | tf_op jit(solution)/shard_map/ppermute | solution.py:20
  95.1 8.9 %collective-permute-start.12 = (f32[54,16,1]{2,1,0:T(8,128)S(1)}, f32[54,16,1]{2,1,0:T(8,128)S(1)}, u32[]{:S(2)}, u32[]{:S(2)}) collective-permute-start(f32[54,16,1]{2,1,0:T(8,128)S(1)} %get-tuple-element.16), channel_id=1, source_target_pairs={{0,1},{1,2},{2,3},{3,4},{4,5},{5,6},{6,7},{7,8},{8,9},{9,10},{10,1... | collective-permute-start | bytes 10376 | tf_op jit(solution)/shard_map/ppermute | solution.py:20
  95.1 8.9 %collective-permute-start.13 = (f32[54,16,1]{2,1,0:T(8,128)S(1)}, f32[54,16,1]{2,1,0:T(8,128)S(1)}, u32[]{:S(2)}, u32[]{:S(2)}) collective-permute-start(f32[54,16,1]{2,1,0:T(8,128)S(1)} %get-tuple-element.17), channel_id=1, source_target_pairs={{1,0},{2,1},{3,2},{4,3},{5,4},{6,5},{7,6},{8,7},{9,8},{10,9},{11,1... | collective-permute-start | bytes 10376 | tf_op jit(solution)/shard_map/ppermute | solution.py:21
  104.5 101.4 %collective-permute-start.14 = (f32[54,1,130]{2,1,0:T(1,128)S(1)}, f32[54,1,130]{2,1,0:T(1,128)S(1)}, u32[]{:S(2)}, u32[]{:S(2)}) collective-permute-start(f32[54,1,130]{2,1,0:T(1,128)S(1)} %get-tuple-element.12), channel_id=1, source_target_pairs={{16,0},{32,16},{48,32},{64,48},{80,64},{96,80},{112,96},{17,1},{33... | collective-permute-start | bytes 84248 | tf_op jit(solution)/shard_map/ppermute | solution.py:21
  106.4 99.5 %collective-permute-start.15 = (f32[54,1,130]{2,1,0:T(1,128)S(1)}, f32[54,1,130]{2,1,0:T(1,128)S(1)}, u32[]{:S(2)}, u32[]{:S(2)}) collective-permute-start(f32[54,1,130]{2,1,0:T(1,128)S(1)} %get-tuple-element.13), channel_id=1, source_target_pairs={{0,16},{16,32},{32,48},{48,64},{64,80},{80,96},{96,112},{1,17},{17... | collective-permute-start | bytes 84248 | tf_op jit(solution)/shard_map/ppermute | solution.py:20
  205.1 86.4 %all-reduce.5.cloned.1.call-start = ((), (), s32[]{:S(2)}) async-start(), calls=%async_computation.1 | async-start | bytes 196608 | tf_op jit(solution)/shard_map/psum | solution.py:170
  205.9 89.2 %copy-start.16 = (f32[24064]{0:T(1024)S(1)}, f32[24064]{0:T(1024)}, u32[]{:S(2)}) copy-start(f32[24064]{0:T(1024)} %param.17) | copy-start | bytes 288772
  226.9 68.2 %copy-start.8 = (bf16[128,128]{1,0:T(8,128)(2,1)S(1)}, bf16[128,128]{1,0:T(8,128)(2,1)}, u32[]{:S(2)}) copy-start(bf16[128,128]{1,0:T(8,128)(2,1)} %param.14) | copy-start | bytes 98308
  (15 other events, 34.2 us)
Sparse Core Ops, SparseCore 0:
  98.9 104.6 all-reduce.2
  209.1 82.3 all-reduce.4
where the time goes:
time: 306 us; the launch traced here: 305 us
  waiting for transfers between devices  184 us (60%)
  starting transfers between devices  42.6 us (14%)
  local copies, waits for them, and re-layouts  20.1 us (7%)
  blocking collectives  20.1 us (7%)
  between operations  17.7 us (6%)
  other arithmetic  10.5 us (3%)
  matrix products  9.52 us (3%)
    psum x1, waiting for transfers between devices, on_device(): band = lax.psum(local_grad, 'lon')  93.3 us
    psum x1, waiting for transfers between devices, on_device(): total_grad, band_square = lax.psum((band, jnp.sum(band * band)), 'lat')  64.6 us
    ppermute x8, starting transfers between devices, with_halo(): after = lax.ppermute(first, axis, down)  28.7 us
    ppermute x8, waiting for transfers between devices, with_halo(): before = lax.ppermute(last, axis, up)  25.5 us
    psum x1, blocking collectives, on_device(): total_grad, band_square = lax.psum((band, jnp.sum(band * band)), 'lat')  20.1 us
    ppermute x8, starting transfers between devices, with_halo(): before = lax.ppermute(last, axis, up)  13.9 us
    concatenate x2, local copies, waits for them, and re-layouts, backward_block(): jnp.concatenate([blank, spread, blank, spread, direct - 4.0 * spread, spr...  12.4 us
  transfers between devices with their start and end apart: 18, of which 9 were waited for; matrix products, arithmetic and copies ran while one was open for 2% of the time, Pallas kernels for 0%

commit v1 on v0

--- a/solution.py
+++ b/solution.py
@@ -166,7 +166,10 @@
             )
         adjoint = total
     params_count = local_grad.shape[0]
-    band = lax.psum(local_grad, "lon")
+    peers, band = (lax.axis_size("lon"), local_grad)
+    for stride in [1 << k for k in range(peers.bit_length() - 1)]:
+        route = [(i_2, i_2 ^ stride) for i_2 in range(peers)]
+        band = band + lax.ppermute(band, "lon", route)
     total_grad, band_square = lax.psum((band, jnp.sum(band * band)), "lat")
     grad_square = jnp.sum(total_grad * total_grad)
     noise_ratio = (band_square / (grad_square + epsilon)).reshape(1)

time: 306 us -> 221 us (0.72)
  waiting for transfers between devices: 184 us -> 91.7 us
  starting transfers between devices: 42.6 us -> 54.2 us
  blocking collectives: 20.1 us -> 16.6 us
    psum x1 -> x0, waiting for transfers between devices: 93.3 us -> none  [on_device(): band = lax.psum(local_grad, 'lon')]
    ppermute x0 -> x4, starting transfers between devices: none -> 11.6 us  [on_device(): band = band + lax.ppermute(band, 'lon', route)]
    ppermute x0 -> x4, waiting for transfers between devices: none -> 9.5 us  [on_device(): band = band + lax.ppermute(band, 'lon', route)]
    psum x1, waiting for transfers between devices: 64.6 us -> 59.1 us  [on_device(): total_grad, band_square = lax.psum((band, jnp.sum(band * band)), 'lat')]
    psum x1, blocking collectives: 20.1 us -> 16.6 us  [on_device(): total_grad, band_square = lax.psum((band, jnp.sum(band * band)), 'lat')]
  transfers between devices with their start and end apart: 18 -> 21, of which waited for: 9 -> 12; matrix products, arithmetic and copies ran while one was open for 2% -> 3% of each run, Pallas kernels for 0% -> 0%
where the time goes in v1:
time: 221 us; the launch traced here: 219 us
  waiting for transfers between devices  91.7 us (41%)
  starting transfers between devices  54.2 us (25%)
  local copies, waits for them, and re-layouts  20.7 us (9%)
  between operations  17.7 us (8%)
  blocking collectives  16.6 us (8%)
  matrix products  9.54 us (4%)
  other arithmetic  8.75 us (4%)
    psum x1, waiting for transfers between devices, on_device(): total_grad, band_square = lax.psum((band, jnp.sum(band * band)), 'lat')  59.1 us
    ppermute x8, starting transfers between devices, with_halo(): after = lax.ppermute(first, axis, down)  28.3 us
    ppermute x8, waiting for transfers between devices, with_halo(): before = lax.ppermute(last, axis, up)  23.1 us
    psum x1, blocking collectives, on_device(): total_grad, band_square = lax.psum((band, jnp.sum(band * band)), 'lat')  16.6 us
    ppermute x8, starting transfers between devices, with_halo(): before = lax.ppermute(last, axis, up)  14.2 us
    concatenate x2, local copies, waits for them, and re-layouts, backward_block(): jnp.concatenate([blank, spread, blank, spread, direct - 4.0 * spread, spr...  12.5 us
    ppermute x4, starting transfers between devices, on_device(): band = band + lax.ppermute(band, 'lon', route)  11.6 us
    ppermute x4, waiting for transfers between devices, on_device(): band = band + lax.ppermute(band, 'lon', route)  9.5 us
  transfers between devices with their start and end apart: 21, of which 12 were waited for; matrix products, arithmetic and copies ran while one was open for 3% of the time, Pallas kernels for 0%

profile of v1, /device:TPU:40, one launch (start us, length us, event | category | flops | bytes accessed | tf_op | source)
XLA Modules:
  0.0 219.3 jit_solution(8801766002592100456)
XLA Ops:
  8.2 8.5 %collective-permute-start.1 = (f32[6,16,1]{2,1,0:T(8,128)S(1)}, f32[6,16,1]{2,1,0:T(8,128)S(1)}, u32[]{:S(2)}, u32[]{:S(2)}) collective-permute-start(f32[6,16,1]{2,1,0:T(8,128)S(1)} %get-tuple-element.33), channel_id=1, source_target_pairs={{1,0},{2,1},{3,2},{4,3},{5,4},{6,5},{7,6},{8,7},{9,8},{10,9},{11,1... | collective-permute-start | bytes 1160 | tf_op jit(solution)/shard_map/ppermute | solution.py:21
  18.6 5.5 %collective-permute-start.3 = (f32[6,1,130]{2,1,0:T(1,128)S(1)}, f32[6,1,130]{2,1,0:T(1,128)S(1)}, u32[]{:S(2)}, u32[]{:S(2)}) collective-permute-start(f32[6,1,130]{2,1,0:T(1,128)S(1)} %get-tuple-element.28), channel_id=1, source_target_pairs={{16,0},{32,16},{48,32},{64,48},{80,64},{96,80},{112,96},{17,1},{33... | collective-permute-start | bytes 9368 | tf_op jit(solution)/shard_map/ppermute | solution.py:21
  24.0 1.9 collective-permute-start.2
  26.7 5.0 %collective-permute-done.2 = f32[6,1,130]{2,1,0:T(1,128)S(1)} collective-permute-done((f32[6,1,130]{2,1,0:T(1,128)S(1)}, f32[6,1,130]{2,1,0:T(1,128)S(1)}, u32[]{:S(2)}, u32[]{:S(2)}) %collective-permute-start.2) | collective-permute-done | bytes 3152 | tf_op jit(solution)/shard_map/ppermute | solution.py:20
  35.5 3.0 %collective-permute-start.5 = (f32[6,16,1]{2,1,0:T(8,128)S(1)}, f32[6,16,1]{2,1,0:T(8,128)S(1)}, u32[]{:S(2)}, u32[]{:S(2)}) collective-permute-start(f32[6,16,1]{2,1,0:T(8,128)S(1)} %get-tuple-element.31), channel_id=1, source_target_pairs={{1,0},{2,1},{3,2},{4,3},{5,4},{6,5},{7,6},{8,7},{9,8},{10,9},{11,1... | collective-permute-start | bytes 1160 | tf_op jit(solution)/shard_map/ppermute | solution.py:21
  40.4 1.9 collective-permute-start.7
  42.3 3.9 %collective-permute-start.6 = (f32[6,1,130]{2,1,0:T(1,128)S(1)}, f32[6,1,130]{2,1,0:T(1,128)S(1)}, u32[]{:S(2)}, u32[]{:S(2)}) collective-permute-start(f32[6,1,130]{2,1,0:T(1,128)S(1)} %get-tuple-element.25), channel_id=1, source_target_pairs={{0,16},{16,32},{32,48},{48,64},{64,80},{80,96},{96,112},{1,17},{17... | collective-permute-start | bytes 9368 | tf_op jit(solution)/shard_map/ppermute | solution.py:20
  46.5 3.5 %collective-permute-done.6 = f32[6,1,130]{2,1,0:T(1,128)S(1)} collective-permute-done((f32[6,1,130]{2,1,0:T(1,128)S(1)}, f32[6,1,130]{2,1,0:T(1,128)S(1)}, u32[]{:S(2)}, u32[]{:S(2)}) %collective-permute-start.6) | collective-permute-done | bytes 3152 | tf_op jit(solution)/shard_map/ppermute | solution.py:20
  56.4 11.9 %concatenate.120 = f32[54,2048]{1,0:T(8,128)} concatenate(f32[6,2048]{1,0:T(8,128)S(1)} %broadcast.26, f32[6,2048]{1,0:T(8,128)S(1)} %bitcast_multiply_fusion.2, f32[6,2048]{1,0:T(8,128)S(1)} %broadcast.26, f32[6,2048]{1,0:T(8,128)S(1)} %bitcast_multiply_fusion.2, f32[6,2048]{1,0:T(8,128)} %fusion.13, f32[6,2048]{1,0:T(8,128)S(1)} %bitcast_multiply_fusion.2, ...), dimensions={0} | concatenate | bytes 884736 | tf_op jit(solution)/shard_map/concatenate | solution.py:112
  70.1 2.9 %collective-permute-start.9 = (f32[54,16,1]{2,1,0:T(8,128)S(1)}, f32[54,16,1]{2,1,0:T(8,128)S(1)}, u32[]{:S(2)}, u32[]{:S(2)}) collective-permute-start(f32[54,16,1]{2,1,0:T(8,128)S(1)} %get-tuple-element.21), channel_id=1, source_target_pairs={{1,0},{2,1},{3,2},{4,3},{5,4},{6,5},{7,6},{8,7},{9,8},{10,9},{11,1... | collective-permute-start | bytes 10376 | tf_op jit(solution)/shard_map/ppermute | solution.py:21
  74.1 5.0 %collective-permute-done.8 = f32[54,16,1]{2,1,0:T(8,128)S(1)} collective-permute-done((f32[54,16,1]{2,1,0:T(8,128)S(1)}, f32[54,16,1]{2,1,0:T(8,128)S(1)}, u32[]{:S(2)}, u32[]{:S(2)}) %collective-permute-start.8) | collective-permute-done | bytes 3488 | tf_op jit(solution)/shard_map/ppermute | solution.py:20
  80.1 2.0 collective-permute-start.10
  82.2 4.1 %collective-permute-start.11 = (f32[54,1,130]{2,1,0:T(1,128)}, f32[54,1,130]{2,1,0:T(1,128)}, u32[]{:S(2)}, u32[]{:S(2)}) collective-permute-start(f32[54,1,130]{2,1,0:T(1,128)} %get-tuple-element.17), channel_id=1, source_target_pairs={{0,16},{16,32},{32,48},{48,64},{64,80},{80,96},{96,112},{1,17},{17... | collective-permute-start | bytes 84248 | tf_op jit(solution)/shard_map/ppermute | solution.py:20
  86.6 4.2 %collective-permute-done.11 = f32[54,1,130]{2,1,0:T(1,128)} collective-permute-done((f32[54,1,130]{2,1,0:T(1,128)}, f32[54,1,130]{2,1,0:T(1,128)}, u32[]{:S(2)}, u32[]{:S(2)}) %collective-permute-start.11) | collective-permute-done | bytes 28112 | tf_op jit(solution)/shard_map/ppermute | solution.py:20
  94.5 1.9 collective-permute-start.16
  97.7 1.9 collective-permute-start.17
  100.2 2.6 %collective-permute-start.13 = (f32[54,16,1]{2,1,0:T(8,128)S(1)}, f32[54,16,1]{2,1,0:T(8,128)S(1)}, u32[]{:S(2)}, u32[]{:S(2)}) collective-permute-start(f32[54,16,1]{2,1,0:T(8,128)S(1)} %get-tuple-element.19), channel_id=1, source_target_pairs={{1,0},{2,1},{3,2},{4,3},{5,4},{6,5},{7,6},{8,7},{9,8},{10,9},{11,1... | collective-permute-start | bytes 10376 | tf_op jit(solution)/shard_map/ppermute | solution.py:21
  104.7 3.4 %collective-permute-start.18 = (f32[24064]{0:T(1024)S(1)}, f32[24064]{0:T(1024)S(1)}, u32[]{:S(2)}, u32[]{:S(2)}) collective-permute-start(f32[24064]{0:T(1024)S(1)} %add.162), channel_id=1, source_target_pairs={{0,4},{1,5},{2,6},{3,7},{4,0},{5,1},{6,2},{7,3},{8,12},{9,13},{10,... | collective-permute-start | bytes 288776 | tf_op jit(solution)/shard_map/ppermute | solution.py:172
  108.2 7.3 %collective-permute-done.18 = f32[24064]{0:T(1024)S(1)} collective-permute-done((f32[24064]{0:T(1024)S(1)}, f32[24064]{0:T(1024)S(1)}, u32[]{:S(2)}, u32[]{:S(2)}) %collective-permute-start.18) | collective-permute-done | bytes 96288 | tf_op jit(solution)/shard_map/ppermute | solution.py:172
  115.5 4.4 %collective-permute-start.19 = (f32[24064]{0:T(1024)S(1)}, f32[24064]{0:T(1024)S(1)}, u32[]{:S(2)}, u32[]{:S(2)}) collective-permute-start(f32[24064]{0:T(1024)S(1)} %add.163), channel_id=1, source_target_pairs={{0,8},{1,9},{2,10},{3,11},{4,12},{5,13},{6,14},{7,15},{8,0},{9,1},... | collective-permute-start | bytes 288776 | tf_op jit(solution)/shard_map/ppermute | solution.py:172
  122.2 3.9 %collective-permute-start.15 = (f32[54,1,130]{2,1,0:T(1,128)S(1)}, f32[54,1,130]{2,1,0:T(1,128)S(1)}, u32[]{:S(2)}, u32[]{:S(2)}) collective-permute-start(f32[54,1,130]{2,1,0:T(1,128)S(1)} %get-tuple-element.15), channel_id=1, source_target_pairs={{0,16},{16,32},{32,48},{48,64},{64,80},{80,96},{96,112},{1,17},{17... | collective-permute-start | bytes 84248 | tf_op jit(solution)/shard_map/ppermute | solution.py:20
  127.6 2.8 %collective-permute-done.15 = f32[54,1,130]{2,1,0:T(1,128)S(1)} collective-permute-done((f32[54,1,130]{2,1,0:T(1,128)S(1)}, f32[54,1,130]{2,1,0:T(1,128)S(1)}, u32[]{:S(2)}, u32[]{:S(2)}) %collective-permute-start.15) | collective-permute-done | bytes 28112 | tf_op jit(solution)/shard_map/ppermute | solution.py:20
  131.3 16.6 %psum.15 = f32[]{:T(128)} all-reduce(f32[]{:T(128)} %get-tuple-element.4), channel_id=1, replica_groups=mesh['ens'=4,'lat'=8,'lon'=16] {'lat'}, use_global_device_ids=true, to_apply=%region_3.0 | all-reduce | flops 1 | bytes 8 | tf_op jit(solution)/shard_map/psum | solution.py:173
  147.9 59.1 %all-reduce.2.cloned.1.call-done = f32[24064]{0:T(1024)} async-done(((f32[24064]{0:T(1024)}), f32[24064]{0:T(1024)}) %all-reduce.2.cloned.1.call-update) | async-done | bytes 96272 | tf_op jit(solution)/shard_map/psum | solution.py:173
  (143 shorter events, 34.3 us)
Async XLA Ops:
  7.2 199.9 %all-reduce.2.cloned.1.call-start = ((), (), s32[]{:S(2)}) async-start(), calls=%async_computation | async-start | bytes 196608 | tf_op jit(solution)/shard_map/psum | solution.py:173
  8.2 10.3 %collective-permute-start = (f32[6,16,1]{2,1,0:T(8,128)S(1)}, f32[6,16,1]{2,1,0:T(8,128)S(1)}, u32[]{:S(2)}, u32[]{:S(2)}) collective-permute-start(f32[6,16,1]{2,1,0:T(8,128)S(1)} %get-tuple-element.32), channel_id=1, source_target_pairs={{0,1},{1,2},{2,3},{3,4},{4,5},{5,6},{6,7},{7,8},{8,9},{9,10},{10,1... | collective-permute-start | bytes 1160 | tf_op jit(solution)/shard_map/ppermute | solution.py:20
  8.2 10.2 %collective-permute-start.1 = (f32[6,16,1]{2,1,0:T(8,128)S(1)}, f32[6,16,1]{2,1,0:T(8,128)S(1)}, u32[]{:S(2)}, u32[]{:S(2)}) collective-permute-start(f32[6,16,1]{2,1,0:T(8,128)S(1)} %get-tuple-element.33), channel_id=1, source_target_pairs={{1,0},{2,1},{3,2},{4,3},{5,4},{6,5},{7,6},{8,7},{9,8},{10,9},{11,1... | collective-permute-start | bytes 1160 | tf_op jit(solution)/shard_map/ppermute | solution.py:21
  18.6 8.1 %collective-permute-start.3 = (f32[6,1,130]{2,1,0:T(1,128)S(1)}, f32[6,1,130]{2,1,0:T(1,128)S(1)}, u32[]{:S(2)}, u32[]{:S(2)}) collective-permute-start(f32[6,1,130]{2,1,0:T(1,128)S(1)} %get-tuple-element.28), channel_id=1, source_target_pairs={{16,0},{32,16},{48,32},{64,48},{80,64},{96,80},{112,96},{17,1},{33... | collective-permute-start | bytes 9368 | tf_op jit(solution)/shard_map/ppermute | solution.py:21
  24.0 7.6 %collective-permute-start.2 = (f32[6,1,130]{2,1,0:T(1,128)S(1)}, f32[6,1,130]{2,1,0:T(1,128)S(1)}, u32[]{:S(2)}, u32[]{:S(2)}) collective-permute-start(f32[6,1,130]{2,1,0:T(1,128)S(1)} %get-tuple-element.29), channel_id=1, source_target_pairs={{0,16},{16,32},{32,48},{48,64},{64,80},{80,96},{96,112},{1,17},{17... | collective-permute-start | bytes 9368 | tf_op jit(solution)/shard_map/ppermute | solution.py:20
  26.7 25.1 %copy-start.14 = (f32[16,128]{1,0:T(8,128)}, f32[16,128]{1,0:T(8,128)S(1)}, u32[]{:S(2)}) copy-start(f32[16,128]{1,0:T(8,128)S(1)} %convert_element_type.70) | copy-start | bytes 24580
  35.5 4.7 %collective-permute-start.4 = (f32[6,16,1]{2,1,0:T(8,128)S(1)}, f32[6,16,1]{2,1,0:T(8,128)S(1)}, u32[]{:S(2)}, u32[]{:S(2)}) collective-permute-start(f32[6,16,1]{2,1,0:T(8,128)S(1)} %get-tuple-element.30), channel_id=1, source_target_pairs={{0,1},{1,2},{2,3},{3,4},{4,5},{5,6},{6,7},{7,8},{8,9},{9,10},{10,1... | collective-permute-start | bytes 1160 | tf_op jit(solution)/shard_map/ppermute | solution.py:20
  35.5 4.7 %collective-permute-start.5 = (f32[6,16,1]{2,1,0:T(8,128)S(1)}, f32[6,16,1]{2,1,0:T(8,128)S(1)}, u32[]{:S(2)}, u32[]{:S(2)}) collective-permute-start(f32[6,16,1]{2,1,0:T(8,128)S(1)} %get-tuple-element.31), channel_id=1, source_target_pairs={{1,0},{2,1},{3,2},{4,3},{5,4},{6,5},{7,6},{8,7},{9,8},{10,9},{11,1... | collective-permute-start | bytes 1160 | tf_op jit(solution)/shard_map/ppermute | solution.py:21
  40.4 6.1 %collective-permute-start.7 = (f32[6,1,130]{2,1,0:T(1,128)S(1)}, f32[6,1,130]{2,1,0:T(1,128)S(1)}, u32[]{:S(2)}, u32[]{:S(2)}) collective-permute-start(f32[6,1,130]{2,1,0:T(1,128)S(1)} %get-tuple-element.24), channel_id=1, source_target_pairs={{16,0},{32,16},{48,32},{64,48},{80,64},{96,80},{112,96},{17,1},{33... | collective-permute-start | bytes 9368 | tf_op jit(solution)/shard_map/ppermute | solution.py:21
  42.3 7.6 %collective-permute-start.6 = (f32[6,1,130]{2,1,0:T(1,128)S(1)}, f32[6,1,130]{2,1,0:T(1,128)S(1)}, u32[]{:S(2)}, u32[]{:S(2)}) collective-permute-start(f32[6,1,130]{2,1,0:T(1,128)S(1)} %get-tuple-element.25), channel_id=1, source_target_pairs={{0,16},{16,32},{32,48},{48,64},{64,80},{80,96},{96,112},{1,17},{17... | collective-permute-start | bytes 9368 | tf_op jit(solution)/shard_map/ppermute | solution.py:20
  70.1 8.9 %collective-permute-start.8 = (f32[54,16,1]{2,1,0:T(8,128)S(1)}, f32[54,16,1]{2,1,0:T(8,128)S(1)}, u32[]{:S(2)}, u32[]{:S(2)}) collective-permute-start(f32[54,16,1]{2,1,0:T(8,128)S(1)} %get-tuple-element.20), channel_id=1, source_target_pairs={{0,1},{1,2},{2,3},{3,4},{4,5},{5,6},{6,7},{7,8},{8,9},{9,10},{10,1... | collective-permute-start | bytes 10376 | tf_op jit(solution)/shard_map/ppermute | solution.py:20
  70.1 8.9 %collective-permute-start.9 = (f32[54,16,1]{2,1,0:T(8,128)S(1)}, f32[54,16,1]{2,1,0:T(8,128)S(1)}, u32[]{:S(2)}, u32[]{:S(2)}) collective-permute-start(f32[54,16,1]{2,1,0:T(8,128)S(1)} %get-tuple-element.21), channel_id=1, source_target_pairs={{1,0},{2,1},{3,2},{4,3},{5,4},{6,5},{7,6},{8,7},{9,8},{10,9},{11,1... | collective-permute-start | bytes 10376 | tf_op jit(solution)/shard_map/ppermute | solution.py:21
  80.1 6.5 %collective-permute-start.10 = (f32[54,1,130]{2,1,0:T(1,128)}, f32[54,1,130]{2,1,0:T(1,128)S(1)}, u32[]{:S(2)}, u32[]{:S(2)}) collective-permute-start(f32[54,1,130]{2,1,0:T(1,128)} %get-tuple-element.16), channel_id=1, source_target_pairs={{16,0},{32,16},{48,32},{64,48},{80,64},{96,80},{112,96},{17,1},{33... | collective-permute-start | bytes 84248 | tf_op jit(solution)/shard_map/ppermute | solution.py:21
  82.2 8.6 %collective-permute-start.11 = (f32[54,1,130]{2,1,0:T(1,128)}, f32[54,1,130]{2,1,0:T(1,128)}, u32[]{:S(2)}, u32[]{:S(2)}) collective-permute-start(f32[54,1,130]{2,1,0:T(1,128)} %get-tuple-element.17), channel_id=1, source_target_pairs={{0,16},{16,32},{32,48},{48,64},{64,80},{80,96},{96,112},{1,17},{17... | collective-permute-start | bytes 84248 | tf_op jit(solution)/shard_map/ppermute | solution.py:20
  94.5 3.2 %collective-permute-start.16 = (f32[24064]{0:T(1024)S(1)}, f32[24064]{0:T(1024)S(1)}, u32[]{:S(2)}, u32[]{:S(2)}) collective-permute-start(f32[24064]{0:T(1024)S(1)} %maximum_add_fusion), channel_id=1, source_target_pairs={{0,1},{1,0},{2,3},{3,2},{4,5},{5,4},{6,7},{7,6},{8,9},{9,8},{10,11... | collective-permute-start | bytes 288776 | tf_op jit(solution)/shard_map/ppermute | solution.py:172
  97.7 7.0 %collective-permute-start.17 = (f32[24064]{0:T(1024)S(1)}, f32[24064]{0:T(1024)S(1)}, u32[]{:S(2)}, u32[]{:S(2)}) collective-permute-start(f32[24064]{0:T(1024)S(1)} %add.161), channel_id=1, source_target_pairs={{0,2},{1,3},{2,0},{3,1},{4,6},{5,7},{6,4},{7,5},{8,10},{9,11},{10,... | collective-permute-start | bytes 288776 | tf_op jit(solution)/shard_map/ppermute | solution.py:172
  99.8 20.0 %collective-permute-start.12 = (f32[54,16,1]{2,1,0:T(8,128)S(1)}, f32[54,16,1]{2,1,0:T(8,128)S(1)}, u32[]{:S(2)}, u32[]{:S(2)}) collective-permute-start(f32[54,16,1]{2,1,0:T(8,128)S(1)} %get-tuple-element.18), channel_id=1, source_target_pairs={{0,1},{1,2},{2,3},{3,4},{4,5},{5,6},{6,7},{7,8},{8,9},{9,10},{10,1... | collective-permute-start | bytes 10376 | tf_op jit(solution)/shard_map/ppermute | solution.py:20
  100.2 19.7 %collective-permute-start.13 = (f32[54,16,1]{2,1,0:T(8,128)S(1)}, f32[54,16,1]{2,1,0:T(8,128)S(1)}, u32[]{:S(2)}, u32[]{:S(2)}) collective-permute-start(f32[54,16,1]{2,1,0:T(8,128)S(1)} %get-tuple-element.19), channel_id=1, source_target_pairs={{1,0},{2,1},{3,2},{4,3},{5,4},{6,5},{7,6},{8,7},{9,8},{10,9},{11,1... | collective-permute-start | bytes 10376 | tf_op jit(solution)/shard_map/ppermute | solution.py:21
  104.7 10.8 %collective-permute-start.18 = (f32[24064]{0:T(1024)S(1)}, f32[24064]{0:T(1024)S(1)}, u32[]{:S(2)}, u32[]{:S(2)}) collective-permute-start(f32[24064]{0:T(1024)S(1)} %add.162), channel_id=1, source_target_pairs={{0,4},{1,5},{2,6},{3,7},{4,0},{5,1},{6,2},{7,3},{8,12},{9,13},{10,... | collective-permute-start | bytes 288776 | tf_op jit(solution)/shard_map/ppermute | solution.py:172
  115.5 10.8 %collective-permute-start.19 = (f32[24064]{0:T(1024)S(1)}, f32[24064]{0:T(1024)S(1)}, u32[]{:S(2)}, u32[]{:S(2)}) collective-permute-start(f32[24064]{0:T(1024)S(1)} %add.163), channel_id=1, source_target_pairs={{0,8},{1,9},{2,10},{3,11},{4,12},{5,13},{6,14},{7,15},{8,0},{9,1},... | collective-permute-start | bytes 288776 | tf_op jit(solution)/shard_map/ppermute | solution.py:172
  120.3 7.3 %collective-permute-start.14 = (f32[54,1,130]{2,1,0:T(1,128)S(1)}, f32[54,1,130]{2,1,0:T(1,128)S(1)}, u32[]{:S(2)}, u32[]{:S(2)}) collective-permute-start(f32[54,1,130]{2,1,0:T(1,128)S(1)} %get-tuple-element.14), channel_id=1, source_target_pairs={{16,0},{32,16},{48,32},{64,48},{80,64},{96,80},{112,96},{17,1},{33... | collective-permute-start | bytes 84248 | tf_op jit(solution)/shard_map/ppermute | solution.py:21
  122.2 8.2 %collective-permute-start.15 = (f32[54,1,130]{2,1,0:T(1,128)S(1)}, f32[54,1,130]{2,1,0:T(1,128)S(1)}, u32[]{:S(2)}, u32[]{:S(2)}) collective-permute-start(f32[54,1,130]{2,1,0:T(1,128)S(1)} %get-tuple-element.15), channel_id=1, source_target_pairs={{0,16},{16,32},{32,48},{48,64},{64,80},{80,96},{96,112},{1,17},{17... | collective-permute-start | bytes 84248 | tf_op jit(solution)/shard_map/ppermute | solution.py:20
  130.4 80.2 %copy-start.16 = (f32[24064]{0:T(1024)S(1)}, f32[24064]{0:T(1024)}, u32[]{:S(2)}) copy-start(f32[24064]{0:T(1024)} %param.17) | copy-start | bytes 288772
  131.3 79.4 %copy-start.17 = (bf16[6912]{0:T(1024)(128)(2,1)S(1)}, bf16[6912]{0:T(1024)(128)(2,1)}, u32[]{:S(2)}) copy-start(bf16[6912]{0:T(1024)(128)(2,1)} %reshape.86) | copy-start | bytes 41476
  (18 other events, 75.9 us)
Sparse Core Ops, SparseCore 0:
  127.7 79.2 all-reduce.1
